TPU v7x, 32 devices: a whole 2x2x4 slice. The times are simulated.
32 devices in a mesh: section: 2 (over x), ctx: 16 (over z, y, core).
Axes of the slice: x: 2, y: 2, z: 4, core: 2. Of those that a mesh axis runs over, the one named last changes fastest.
Arguments:
- resid: bfloat16 [2, 4096, 4096], P('section', 'ctx'), may hold values from -16 to 16
- queries: bfloat16 [2, 4096, 512], P('section', 'ctx'), may hold values from -8 to 8
- keyvals: bfloat16 [2, 4096, 256], P('section', 'ctx'), may hold values from -8 to 8
- run_max: float32 [2, 4096, 4], P('section', 'ctx'), may hold values from 1 to 4
- run_sum: float32 [2, 4096, 4], P('section', 'ctx'), may hold values from 128 to 1024
- run_out: float32 [2, 4096, 512], P('section', 'ctx'), may hold values from -384 to 384
- span_pair: int32 [16, 2], replicated, may hold values from 0 to 31, as said below
- norm_gain: float32 [2, 4096], P('section'), may hold values from 0.5 to 1.5
- w_query: bfloat16 [2, 4096, 512], P('section', 'ctx'), may hold values from -0.095458984 to 0.095458984
- w_keyval: bfloat16 [2, 4096, 256], P('section', 'ctx'), may hold values from -0.095458984 to 0.095458984
- w_out: bfloat16 [2, 512, 4096], P('section', None, 'ctx'), may hold values from -0.59765625 to 0.59765625
Outputs:
- queries_next: bfloat16 [2, 4096, 512], P('section', 'ctx')
- keyvals_next: bfloat16 [2, 4096, 256], P('section', 'ctx')
- max_next: float32 [2, 4096, 4], P('section', 'ctx')
- sum_next: float32 [2, 4096, 4], P('section', 'ctx')
- out_next: float32 [2, 4096, 512], P('section', 'ctx')
Inputs may be any that keep to these rules, and one draw needn't show every extreme that they name: `span_pair`: each ctx index holds blocks c and 31 - c, its first column running once over 0 to 15.
All inputs are finite; a program needn't handle non-finite values.
Results may differ from a plain program's by a relative error of at most 0.005.
The roundings to bfloat16 on the way count: a program that leaves them out, or rounds other values in their place, can miss the bound.
Values may be sent and summed in bfloat16 or wider, within the bound.
A program may use at most 64 MiB of HBM per device.

v0:
```python
import jax
import jax.numpy as jnp
from jax import lax
from jax.sharding import PartitionSpec as P

HEAD = 128
QHEADS = 4


def passed_along(value, axis, steps):
    count = lax.axis_size(axis)
    pairs = [(source, (source + steps) % count) for source in range(count)]
    return lax.ppermute(value, axis, pairs)


def device_positions(span_pair, device, rows_here):
    half_rows = rows_here // 2
    span_row = lax.dynamic_slice_in_dim(span_pair, device, 1, 0)[0]
    offsets = jnp.arange(rows_here, dtype=jnp.int32)
    span_index = jnp.where(offsets < half_rows, span_row[0], span_row[1])
    return span_index * half_rows + offsets % half_rows


def flash_step(query_rows, key_block, pos_query, pos_key, old_max, old_sum, old_out):
    rows_here = query_rows.shape[0]
    query_heads = query_rows.reshape(rows_here, QHEADS, HEAD)
    key_part = key_block[:, :HEAD]
    value_part = key_block[:, HEAD:]
    scores = jnp.einsum(
        "qhd,kd->hqk", query_heads, key_part, preferred_element_type=jnp.float32
    ) * HEAD ** (-0.5)
    keep = pos_key[None, None, :] <= pos_query[None, :, None]
    masked = jnp.where(keep, scores, -1e30)
    prior_max = old_max.T
    new_max = jnp.maximum(prior_max, jnp.max(masked, axis=-1))
    exp_scores = jnp.where(keep, jnp.exp(scores - new_max[:, :, None]), 0.0)
    decay_factor = jnp.exp(prior_max - new_max)
    new_sum = old_sum.T * decay_factor + jnp.sum(exp_scores, axis=-1)
    rounded = exp_scores.astype(jnp.bfloat16)
    contrib = jnp.einsum("hqk,kd->qhd", rounded, value_part, preferred_element_type=jnp.float32)
    new_out = old_out.reshape(rows_here, QHEADS, HEAD) * decay_factor.T[:, :, None] + contrib
    return (new_max.T, new_sum.T, new_out.reshape(rows_here, QHEADS * HEAD))


def add_rows(normed, shard_rows):
    return jnp.dot(normed, shard_rows, preferred_element_type=jnp.float32)


def per_device(
    resid,
    queries,
    keyvals,
    run_max,
    run_sum,
    run_out,
    span_pair,
    norm_gain,
    w_query,
    w_keyval,
    w_out,
):
    cycle_size = lax.axis_size("ctx")
    my_index = lax.axis_index("ctx")
    rows_here = resid.shape[1]
    pos_mine = device_positions(span_pair, my_index, rows_here)
    pos_near = device_positions(span_pair, (my_index + 1) % cycle_size, rows_here)
    pos_far = device_positions(span_pair, (my_index + 2) % cycle_size, rows_here)
    keyval_own = keyvals[0]
    near_block = passed_along(keyval_own, "ctx", -1)
    far_block = passed_along(near_block, "ctx", -1)
    max_now, sum_now, out_now = flash_step(
        queries[0], far_block, pos_mine, pos_far, run_max[0], run_sum[0], run_out[0]
    )
    max_now, sum_now, out_now = flash_step(
        queries[0], near_block, pos_mine, pos_near, max_now, sum_now, out_now
    )
    divided = out_now.reshape(rows_here, QHEADS, HEAD) / sum_now[:, :, None]
    attended = divided.reshape(rows_here, QHEADS * HEAD).astype(jnp.bfloat16)
    projected = jnp.dot(
        attended,
        lax.all_gather(w_out[0], "ctx", axis=1, tiled=True),
        preferred_element_type=jnp.float32,
    )
    finished = (resid[0].astype(jnp.float32) + projected).astype(jnp.bfloat16)
    incoming = passed_along(finished, "section", 1)
    wide = incoming.astype(jnp.float32)
    mean_square = jnp.mean(wide * wide, axis=-1, keepdims=True)
    normed = (wide * lax.rsqrt(mean_square + 1e-05) * norm_gain[0][None, :]).astype(jnp.bfloat16)

    def add_one(shard_rows):
        return add_rows(normed, shard_rows)

    query_sum = add_one(lax.all_gather(w_query[0], "ctx", axis=0, tiled=True))
    keyval_sum = add_one(lax.all_gather(w_keyval[0], "ctx", axis=0, tiled=True))
    query_new = query_sum.astype(jnp.bfloat16)
    keyval_new = keyval_sum.astype(jnp.bfloat16)
    start_max = jnp.full((rows_here, QHEADS), -1e30, jnp.float32)
    start_sum = jnp.zeros((rows_here, QHEADS), jnp.float32)
    start_out = jnp.zeros((rows_here, QHEADS * HEAD), jnp.float32)
    max_new, sum_new, out_new = flash_step(
        query_new, keyval_new, pos_mine, pos_mine, start_max, start_sum, start_out
    )
    return (query_new[None], keyval_new[None], max_new[None], sum_new[None], out_new[None])


def solution(mesh):
    placed = (
        P("section", "ctx", None),
        P("section", "ctx", None),
        P("section", "ctx", None),
        P("section", "ctx", None),
        P("section", "ctx", None),
        P("section", "ctx", None),
        P(),
        P("section", None),
        P("section", "ctx", None),
        P("section", "ctx", None),
        P("section", None, "ctx"),
    )
    return jax.shard_map(
        per_device,
        mesh=mesh,
        in_specs=placed,
        out_specs=(
            P("section", "ctx", None),
            P("section", "ctx", None),
            P("section", "ctx", None),
            P("section", "ctx", None),
            P("section", "ctx", None),
        ),
        check_vma=False,
    )
```

profile of v0, /device:TPU:0, one launch (start us, length us, event | category | flops | bytes accessed | tf_op | source)
XLA Modules:
  0.0 173.9 jit_solution(6768288970073810298)
XLA Ops:
  7.2 0.7 all-gather.7.cloned.1.call-update
  8.0 0.7 all-gather.11.cloned.1.call-update
  8.7 0.7 all-gather.9.cloned.1.call-update
  9.4 5.5 %collective-permute-start = (bf16[256,256]{1,0:T(8,128)(2,1)}, bf16[256,256]{1,0:T(8,128)(2,1)S(1)}, u32[]{:S(2)}, u32[]{:S(2)}) collective-permute-start(bf16[256,256]{1,0:T(8,128)(2,1)} %bitcast.147), channel_id=1, source_target_pairs={{0,15},{1,0},{2,1},{3,2},{4,3},{5,4},{6,5},{7,6},{8,7},{9,8},{10,9... | collective-permute-start | bytes 393224 | tf_op jit(solution)/shard_map/ppermute | solution.py:13
  14.9 1.0 reshape_squeeze.8
  15.9 1.2 copy.16
  17.2 0.9 constant_dynamic-slice_fusion.2
  18.0 0.5 fusion.61
  18.6 1.3 multiply_add_fusion.2
  19.9 0.5 fusion.62
  20.4 0.5 fusion.63
  20.9 2.6 %multiply_add_fusion = (s32[256]{0:T(256)S(1)}, s32[256]{0:T(256)S(1)}) fusion(s32[]{:T(128)} %bitcast.15, s32[]{:T(128)} %bitcast.14, s32[]{:T(128)} %bitcast.6, s32[]{:T(128)} %bitcast.5), kind=kLoop, calls=%fused_computation.81 | loop fusion | flops 3328 | bytes 2064 | tf_op jit(solution)/shard_map/add | solution.py:21
  23.7 0.7 collective-permute-start.1
  24.4 0.3 select_reduce_fusion.1
  24.8 2.2 %collective-permute-done.1 = bf16[256,256]{1,0:T(8,128)(2,1)S(1)} collective-permute-done((bf16[256,256]{1,0:T(8,128)(2,1)S(1)}, bf16[256,256]{1,0:T(8,128)(2,1)S(1)}, u32[]{:S(2)}, u32[]{:S(2)}) %collective-permute-start.1) | collective-permute-done | bytes 131104 | tf_op jit(solution)/shard_map/ppermute | solution.py:13
  26.9 0.3 select_reduce_fusion.2
  27.5 0.2 fusion.26
  27.8 0.3 convolution_bitcast_fusion.1
  28.1 0.4 fusion.17
  28.5 38.9 %all-gather.7.cloned.1.call-done = bf16[1,512,4096]{2,1,0:T(8,128)(2,1)} async-done(((bf16[1,512,256]{2,1,0:T(8,128)(2,1)}), bf16[1,512,4096]{2,1,0:T(8,128)(2,1)}) %all-gather.7.cloned.1.call-update) | async-done | bytes 4194320 | tf_op jit(solution)/shard_map/all_gather | solution.py:81
  67.4 3.5 %fusion = bf16[256,4096]{1,0:T(8,128)(2,1)S(1)} fusion(bf16[256,512]{0,1:T(8,128)(2,1)S(1)} %bitcast.144, bf16[1,512,4096]{2,1,0:T(8,128)(2,1)} %all-gather.7.cloned.1.call-done, bf16[1,256,4096]{2,1,0:T(8,128)(2,1)S(1)} %copy-done), kind=kOutput, calls=%fused_computation.3 | convolution fusion | flops 1076887552 | bytes 8650752 | tf_op jit(solution)/shard_map/dot_general | solution.py:79
  70.9 1.5 collective-permute-start.2
  72.5 46.3 %collective-permute-done.2 = bf16[256,4096]{1,0:T(8,128)(2,1)S(1)} collective-permute-done((bf16[256,4096]{1,0:T(8,128)(2,1)S(1)}, bf16[256,4096]{1,0:T(8,128)(2,1)S(1)}, u32[]{:S(2)}, u32[]{:S(2)}) %collective-permute-start.2) | collective-permute-done | bytes 2097184 | tf_op jit(solution)/shard_map/ppermute | solution.py:13
  118.8 0.5 fusion.1
  119.3 2.4 %fusion.21 = bf16[256,256]{1,0:T(8,128)(2,1)S(1)} fusion(bf16[1,4096,256]{2,1,0:T(8,128)(2,1)} %all-gather.11.cloned.1.call-done, bf16[256,4096]{1,0:T(8,128)(2,1)S(1)} %collective-permute-done.2, f32[4096]{0:T(1024)S(1)} %bitcast.148, f32[256]{0:T(256)S(1)} %add_rsqrt_fusion), kind=kOutput, calls=%fused_computation.28 | convolution fusion | flops 541130752 | bytes 4342784 | tf_op jit(solution)/shard_map/dot_general | solution.py:46
  121.7 39.0 %all-gather.9.cloned.1.call-done = bf16[1,4096,512]{2,1,0:T(8,128)(2,1)} async-done(((bf16[1,256,512]{2,1,0:T(8,128)(2,1)}), bf16[1,4096,512]{2,1,0:T(8,128)(2,1)}) %all-gather.9.cloned.1.call-update) | async-done | bytes 4194320 | tf_op jit(solution)/shard_map/all_gather | solution.py:93
  160.8 3.5 %fusion.18 = bf16[256,512]{1,0:T(8,128)(2,1)S(1)} fusion(bf16[1,4096,512]{2,1,0:T(8,128)(2,1)} %all-gather.9.cloned.1.call-done, bf16[256,4096]{1,0:T(8,128)(2,1)S(1)} %collective-permute-done.2, f32[4096]{0:T(1024)S(1)} %bitcast.149, f32[256]{0:T(256)S(1)} %add_rsqrt_fusion), kind=kOutput, calls=%fused_computation.27 | convolution fusion | flops 1078067200 | bytes 6571008 | tf_op jit(solution)/shard_map/dot_general | solution.py:46
  164.3 0.3 select_reduce_fusion
  164.6 0.6 broadcast_maximum_fusion
  165.4 0.6 fusion.51
  166.0 0.3 fusion.16
  166.4 1.0 copy.26
  (23 shorter events, 0.8 us)
Async XLA Ops:
  7.2 20.1 %copy-start.3 = (f32[1,256,4]{1,2,0:T(4,128)S(1)}, f32[1,256,4]{1,2,0:T(4,128)}, u32[]{:S(2)}) copy-start(f32[1,256,4]{1,2,0:T(4,128)} %param.14) | copy-start | bytes 12292
  7.2 20.6 %copy-start.4 = (f32[1,256,4]{1,2,0:T(4,128)S(1)}, f32[1,256,4]{1,2,0:T(4,128)}, u32[]{:S(2)}) copy-start(f32[1,256,4]{1,2,0:T(4,128)} %param.15) | copy-start | bytes 12292
  7.2 60.2 %all-gather.7.cloned.1.call-start = ((), (), s32[]{:S(2)}) async-start(), calls=%async_computation | async-start | bytes 4456448 | tf_op jit(solution)/shard_map/all_gather | solution.py:81
  7.9 111.4 %all-gather.11.cloned.1.call-start = ((), (), s32[]{:S(2)}) async-start(), calls=%async_computation.2 | async-start | bytes 2228224 | tf_op jit(solution)/shard_map/all_gather | solution.py:94
  8.7 152.1 %all-gather.9.cloned.1.call-start = ((), (), s32[]{:S(2)}) async-start(), calls=%async_computation.1 | async-start | bytes 4456448 | tf_op jit(solution)/shard_map/all_gather | solution.py:93
  9.4 14.3 %collective-permute-start = (bf16[256,256]{1,0:T(8,128)(2,1)}, bf16[256,256]{1,0:T(8,128)(2,1)S(1)}, u32[]{:S(2)}, u32[]{:S(2)}) collective-permute-start(bf16[256,256]{1,0:T(8,128)(2,1)} %bitcast.147), channel_id=1, source_target_pairs={{0,15},{1,0},{2,1},{3,2},{4,3},{5,4},{6,5},{7,6},{8,7},{9,8},{10,9... | collective-permute-start | bytes 393224 | tf_op jit(solution)/shard_map/ppermute | solution.py:13
  23.7 3.2 %collective-permute-start.1 = (bf16[256,256]{1,0:T(8,128)(2,1)S(1)}, bf16[256,256]{1,0:T(8,128)(2,1)S(1)}, u32[]{:S(2)}, u32[]{:S(2)}) collective-permute-start(bf16[256,256]{1,0:T(8,128)(2,1)S(1)} %collective-permute-done), channel_id=1, source_target_pairs={{0,15},{1,0},{2,1},{3,2},{4,3},{5,4},{6,5},{7,6},{8,7},{9,8},{10,9... | collective-permute-start | bytes 393224 | tf_op jit(solution)/shard_map/ppermute | solution.py:13
  27.3 40.1 %copy-start = (bf16[1,256,4096]{2,1,0:T(8,128)(2,1)S(1)}, bf16[1,256,4096]{2,1,0:T(8,128)(2,1)}, u32[]{:S(2)}) copy-start(bf16[1,256,4096]{2,1,0:T(8,128)(2,1)} %param.11) | copy-start | bytes 6291460
  67.4 51.9 %copy-start.5 = (f32[1,4096]{1,0:T(1,128)S(1)}, f32[1,4096]{1,0:T(1,128)}, u32[]{:S(2)}) copy-start(f32[1,4096]{1,0:T(1,128)} %param.18) | copy-start | bytes 49156
  70.9 47.9 %collective-permute-start.2 = (bf16[256,4096]{1,0:T(8,128)(2,1)S(1)}, bf16[256,4096]{1,0:T(8,128)(2,1)S(1)}, u32[]{:S(2)}, u32[]{:S(2)}) collective-permute-start(bf16[256,4096]{1,0:T(8,128)(2,1)S(1)} %fusion), channel_id=1, source_target_pairs={{0,16},{16,0},{1,17},{17,1},{2,18},{18,2},{3,19},{19,3},{4,20},{20... | collective-permute-start | bytes 6291464 | tf_op jit(solution)/shard_map/ppermute | solution.py:13
  121.7 44.3 %copy-start.2 = (bf16[256,256]{1,0:T(8,128)(2,1)}, bf16[256,256]{1,0:T(8,128)(2,1)S(1)}, u32[]{:S(2)}) copy-start(bf16[256,256]{1,0:T(8,128)(2,1)S(1)} %fusion.21) | copy-start | bytes 393220
  164.3 3.1 %copy-start.1 = (bf16[256,512]{1,0:T(8,128)(2,1)}, bf16[256,512]{1,0:T(8,128)(2,1)S(1)}, u32[]{:S(2)}) copy-start(bf16[256,512]{1,0:T(8,128)(2,1)S(1)} %fusion.18) | copy-start | bytes 786436
Sparse Core Ops, SparseCore 0:
  10.2 57.1 all-gather.6
  69.5 39.5 all-gather.10
  111.3 49.4 all-gather.8
where the time goes:
time: 174 us
  waiting for transfers between devices  129 us (74%)
  between operations  13.9 us (8%)
  matrix products  11.4 us (7%)
  starting transfers between devices  7.87 us (5%)
  other arithmetic  6.42 us (4%)
  local copies, waits for them, and re-layouts  5.7 us (3%)
    ppermute x3, waiting for transfers between devices, passed_along(): return lax.ppermute(value, axis, pairs)  48.5 us
    all_gather x1, waiting for transfers between devices, per_device(): query_sum = add_one(lax.all_gather(w_query[0], 'ctx', axis=0, tiled=True))  39 us
    all_gather x1, waiting for transfers between devices, per_device(): lax.all_gather(w_out[0], 'ctx', axis=1, tiled=True)  38.9 us
    ppermute x3, starting transfers between devices, passed_along(): return lax.ppermute(value, axis, pairs)  7.75 us
    dot_general x2, matrix products, add_rows(): return jnp.dot(normed, shard_rows, preferred_element_type=jnp.float32)  5.87 us
    add x2, other arithmetic, device_positions(): return span_index * half_rows + offsets % half_rows  3.89 us
    dot_general x1, matrix products, per_device(): jnp.dot(attended, lax.all_gather(w_out[0], 'ctx', axis=1, tiled=True), pr...  3.54 us
  transfers between devices with their start and end apart: 6, of which 4 were waited for; matrix products, arithmetic and copies ran while one was open for 10% of the time, Pallas kernels for 0%

commit v1 on v0

--- a/solution.py
+++ b/solution.py
@@ -1,10 +1,378 @@
+import functools
+
 import jax
 import jax.numpy as jnp
 from jax import lax
+from jax.experimental import pallas as pl
+from jax.experimental.pallas import tpu as pltpu
 from jax.sharding import PartitionSpec as P
 
 HEAD = 128
 QHEADS = 4
+MESH = pl.DeviceIdType.MESH
+CORE, ACROSS, UP, DOWN = range(4)
+OUT, KV, QA, QB = range(4)
+
+
+def kernel(
+    sections,
+    n,
+    resid_hbm,
+    queries_ref,
+    keyvals_hbm,
+    max_ref,
+    sum_ref,
+    run_ref,
+    span_ref,
+    gain_hbm,
+    wq_hbm,
+    wkv_hbm,
+    wo_hbm,
+    q_out,
+    kv_out,
+    max_out,
+    sum_out,
+    out_out,
+    wo_buf,
+    w_buf,
+    resid_buf,
+    fin_buf,
+    gain_buf,
+    near_buf,
+    att_buf,
+    acc_buf,
+    sq_buf,
+    ship_buf,
+    in_buf,
+    local_sem,
+    send_sem,
+    recv_sem,
+    nsend_sem,
+    nrecv_sem,
+    xsend_sem,
+    gain_sem,
+    rsend_sem,
+    rrecv_sem,
+):
+    sec = lax.axis_index("section")
+    me = lax.axis_index("ctx")
+    layers = n // 4
+    z, y, c = me // 4, (me // 2) % 2, me % 2
+    ahead = lax.rem(sec + 1, sections)
+    behind = lax.rem(sec + sections - 1, sections)
+    rows = resid_buf.shape[0]
+    half = rows // 2
+    unit = w_buf.shape[-1]
+
+    load_resid = pltpu.make_async_copy(resid_hbm.at[0], resid_buf, local_sem.at[0])
+    load_out = pltpu.make_async_copy(wo_hbm.at[0], wo_buf.at[me], local_sem.at[1])
+    load_out.start()
+    load_resid.start()
+
+    def index(zz, yy, cc):
+        return zz * 4 + yy * 2 + cc
+
+    barrier = pltpu.get_barrier_semaphore()
+    fixed = [
+        (sec, index(z, y, 1 - c)),
+        (sec, index(z, 1 - y, c)),
+        (sec, lax.rem(me + 1, n)),
+        (sec, lax.rem(me + 2, n)),
+        (sec, lax.rem(me + n - 1, n)),
+        (sec, lax.rem(me + n - 2, n)),
+        (ahead, me),
+        (behind, me),
+    ]
+    for peer in fixed:
+        pl.semaphore_signal(barrier, inc=1, device_id=peer, device_id_type=MESH)
+
+    @pl.when(z > 0)
+    def _():
+        pl.semaphore_signal(barrier, inc=1, device_id=(sec, me - 4), device_id_type=MESH)
+
+    @pl.when(z < layers - 1)
+    def _():
+        pl.semaphore_signal(barrier, inc=1, device_id=(sec, me + 4), device_id_type=MESH)
+
+    ends = jnp.where(z > 0, 1, 0) + jnp.where(z < layers - 1, 1, 0)
+    pl.semaphore_wait(barrier, len(fixed) + ends)
+
+    def remote(src, dst, send, recv, device):
+        return pltpu.make_async_remote_copy(
+            src_ref=src, dst_ref=dst, send_sem=send, recv_sem=recv,
+            device_id=device, device_id_type=MESH,
+        )
+
+    near_copy = remote(keyvals_hbm.at[0], near_buf.at[0], nsend_sem.at[0], nrecv_sem.at[0],
+                       (sec, lax.rem(me + n - 1, n)))
+    far_copy = remote(keyvals_hbm.at[0], near_buf.at[1], nsend_sem.at[1], nrecv_sem.at[1],
+                      (sec, lax.rem(me + n - 2, n)))
+    near_copy.start()
+    far_copy.start()
+
+    def slot(u, src):
+        return wo_buf.at[src] if u == OUT else w_buf.at[u - 1, src]
+
+    swaps = []
+    for u, ref in ((KV, wkv_hbm.at[0]), (QA, wq_hbm.at[0, :, 0:unit]),
+                   (QB, wq_hbm.at[0, :, unit:2 * unit])):
+        swaps.append(remote(ref, slot(u, me), xsend_sem.at[u], recv_sem.at[u, me], (behind, me)))
+    gain_copy = remote(gain_hbm, gain_buf, xsend_sem.at[0], gain_sem.at[0], (behind, me))
+    swaps[0].start()
+    gain_copy.start()
+
+    def hop(u, src, way):
+        target = {
+            CORE: index(z, y, 1 - c), ACROSS: index(z, 1 - y, c), UP: me + 4, DOWN: me - 4,
+        }[way]
+        return remote(slot(u, src), slot(u, src), send_sem.at[way, u, src],
+                      recv_sem.at[u, src], (sec, target))
+
+    def arrive(u, src):
+        hop(u, src, CORE).wait_recv()
+
+    def each_hop(u, d, other, act, arrived=None):
+        yy = 1 - y if other else y
+
+        def go(src, ways):
+            if arrived is not None:
+                arrived(src)
+            for way in ways:
+                if way == UP:
+                    @pl.when(z < layers - 1)
+                    def _():
+                        act(hop(u, src, UP))
+                elif way == DOWN:
+                    @pl.when(z > 0)
+                    def _():
+                        act(hop(u, src, DOWN))
+                else:
+                    act(hop(u, src, way))
+
+        onward = u == KV or not other
+        across = [ACROSS] if (not other and (u != KV or d == 0)) else []
+        if d == 0:
+            go(index(z, yy, c), ([UP, DOWN] if onward else []) + across + [CORE])
+        else:
+            @pl.when(z >= d)
+            def _():
+                go(index(z - d, yy, c), ([UP] if onward else []) + across + [CORE])
+
+            @pl.when(z + d < layers)
+            def _():
+                go(index(z + d, yy, c), ([DOWN] if onward else []) + across + [CORE])
+
+    def event(u, d, other):
+        own = u == OUT and d == 0 and not other
+        each_hop(u, d, other, lambda copy: copy.start(),
+                 None if own else lambda src: arrive(u, src))
+
+    load_out.wait()
+    event(OUT, 0, False)
+    swaps[1].start()
+    swaps[2].start()
+
+    row = lax.broadcasted_iota(jnp.int32, (rows, 1), 0)
+    col = lax.broadcasted_iota(jnp.int32, (1, rows), 1)
+
+    def position(device, offsets):
+        first, second = span_ref[device, 0], span_ref[device, 1]
+        return jnp.where(offsets < half, first * half + offsets, second * half + offsets - half)
+
+    pos_mine = position(me, row)
+
+    def update(query, key, value, keep, m, l, acc):
+        scores = lax.dot_general(
+            query, key, (((1,), (1,)), ((), ())), preferred_element_type=jnp.float32
+        ) * HEAD ** (-0.5)
+        masked = jnp.where(keep, scores, -1e30)
+        top = jnp.max(masked, axis=1, keepdims=True)
+        m_new = top if m is None else jnp.maximum(m, top)
+        p = jnp.where(keep, jnp.exp(scores - m_new), 0.0)
+        l_new = jnp.sum(p, axis=1, keepdims=True)
+        out = jnp.dot(p.astype(jnp.bfloat16), value, preferred_element_type=jnp.float32)
+        if m is not None:
+            decay = jnp.exp(m - m_new)
+            l_new = l * decay + l_new
+            out = acc * decay + out
+        return m_new, l_new, out
+
+    far_copy.wait_recv()
+    near_copy.wait_recv()
+    keep_far = position(lax.rem(me + 2, n), col) <= pos_mine
+    keep_near = position(lax.rem(me + 1, n), col) <= pos_mine
+
+    def attend(h):
+        cols = slice(h * HEAD, (h + 1) * HEAD)
+        query = queries_ref[0, :, cols]
+        m, l, acc = max_ref[0, :, h:h + 1], sum_ref[0, :, h:h + 1], run_ref[0, :, cols]
+        m, l, acc = update(query, near_buf[1, :, :HEAD], near_buf[1, :, HEAD:], keep_far, m, l, acc)
+        m, l, acc = update(query, near_buf[0, :, :HEAD], near_buf[0, :, HEAD:], keep_near, m, l, acc)
+        att_buf[:, cols] = (acc / l).astype(jnp.bfloat16)
+
+    for h in range(QHEADS):
+        attend(h)
+
+    event(KV, 0, False)
+    event(OUT, 1, False)
+    event(OUT, 0, True)
+    event(KV, 0, True)
+    load_resid.wait()
+    event(OUT, 2, False)
+    event(OUT, 1, True)
+    event(OUT, 3, False)
+    event(QA, 0, False)
+    event(KV, 1, False)
+    event(OUT, 2, True)
+    event(KV, 1, True)
+    event(OUT, 3, True)
+
+    sq_buf[...] = jnp.zeros_like(sq_buf)
+
+    def project(step, carry):
+        src = lax.rem(me + step, n)
+
+        @pl.when(src % 2 != c)
+        def _():
+            arrive(OUT, src)
+
+        at = pl.ds(pl.multiple_of(src * unit, unit), unit)
+        block = jnp.dot(att_buf[...], wo_buf[src], preferred_element_type=jnp.float32)
+        block = (resid_buf[:, at].astype(jnp.float32) + block).astype(jnp.bfloat16)
+        fin_buf[src] = block
+        wide = block.astype(jnp.float32)
+        sq_buf[...] += wide * wide
+        return carry
+
+    lax.fori_loop(0, n, project, 0)
+    gain_copy.wait_recv()
+    mean_square = jnp.sum(sq_buf[...], axis=1, keepdims=True) * (1.0 / (n * unit))
+    inverse = lax.rsqrt(mean_square + 1e-05)
+
+    def normalise(src, carry):
+        at = pl.ds(pl.multiple_of(src * unit, unit), unit)
+        wide = fin_buf[src].astype(jnp.float32)
+        fin_buf[src] = (wide * inverse * gain_buf[:, at]).astype(jnp.bfloat16)
+        return carry
+
+    event(KV, 2, False)
+    event(KV, 2, True)
+    event(QA, 1, False)
+    event(QB, 0, False)
+    lax.fori_loop(0, n, normalise, 0)
+    event(KV, 3, False)
+    event(KV, 3, True)
+    event(QA, 0, True)
+    event(QA, 2, False)
+    event(QA, 1, True)
+
+    def finish(u):
+        acc_buf[...] = jnp.zeros_like(acc_buf)
+
+        def add(src, carry):
+            @pl.when(src % 2 != c)
+            def _():
+                arrive(u, src)
+
+            acc_buf[...] += jnp.dot(fin_buf[src], w_buf[u - 1, src], preferred_element_type=jnp.float32)
+            return carry
+
+        lax.fori_loop(0, n, add, 0)
+        ship_buf[u - 1] = acc_buf[...].astype(jnp.bfloat16)
+        copy = remote(ship_buf.at[u - 1], in_buf.at[u - 1], rsend_sem.at[u - 1],
+                      rrecv_sem.at[u - 1], (ahead, me))
+        copy.start()
+        return copy
+
+    results = [finish(KV)]
+    event(QA, 3, False)
+    event(QB, 1, False)
+    event(QA, 2, True)
+    event(QB, 0, True)
+    event(QB, 2, False)
+    event(QA, 3, True)
+    event(QB, 1, True)
+    event(QB, 3, False)
+    results.append(finish(QA))
+    event(QB, 2, True)
+    event(QB, 3, True)
+    results.append(finish(QB))
+
+    keep_own = position(me, col) <= pos_mine
+
+    def own(h):
+        query = in_buf[1 + h // 2, :, (h % 2) * HEAD:(h % 2 + 1) * HEAD]
+        m, l, acc = update(query, in_buf[0, :, :HEAD], in_buf[0, :, HEAD:], keep_own, None, None, None)
+        max_out[0, :, h:h + 1] = m
+        sum_out[0, :, h:h + 1] = l
+        out_out[0, :, h * HEAD:(h + 1) * HEAD] = acc
+
+    results[0].wait_recv()
+    kv_out[0] = in_buf[0]
+    for pair in range(2):
+        results[1 + pair].wait_recv()
+        q_out[0, :, pair * unit:(pair + 1) * unit] = in_buf[1 + pair]
+        own(2 * pair)
+        own(2 * pair + 1)
+
+    near_copy.wait_send()
+    far_copy.wait_send()
+    gain_copy.wait_send()
+    for copy in swaps + results:
+        copy.wait_send()
+    for u in (OUT, KV, QA, QB):
+        for d in range(layers):
+            for other in (False, True):
+                each_hop(u, d, other, lambda copy: copy.wait_send())
+
+
+def fused(mesh, *args):
+    sections, n = mesh.shape["section"], mesh.shape["ctx"]
+    resid, queries, keyvals, run_max, run_sum, run_out = args[:6]
+    rows, width = resid.shape[1:]
+    unit = keyvals.shape[2]
+    bf16, f32 = jnp.bfloat16, jnp.float32
+    vmem = pl.BlockSpec(memory_space=pltpu.VMEM)
+    smem = pl.BlockSpec(memory_space=pltpu.SMEM)
+    hbm = pl.BlockSpec(memory_space=pl.ANY)
+    dma = pltpu.SemaphoreType.DMA
+    return pl.pallas_call(
+        functools.partial(kernel, sections, n),
+        out_shape=(
+            jax.ShapeDtypeStruct(queries.shape, bf16),
+            jax.ShapeDtypeStruct(keyvals.shape, bf16),
+            jax.ShapeDtypeStruct(run_max.shape, f32),
+            jax.ShapeDtypeStruct(run_sum.shape, f32),
+            jax.ShapeDtypeStruct(run_out.shape, f32),
+        ),
+        in_specs=[hbm, vmem, hbm, vmem, vmem, vmem, smem, hbm, hbm, hbm, hbm],
+        out_specs=[vmem] * 5,
+        scratch_shapes=[
+            pltpu.VMEM((n, 2 * unit, unit), bf16),
+            pltpu.VMEM((3, n, unit, unit), bf16),
+            pltpu.VMEM((rows, width), bf16),
+            pltpu.VMEM((n, rows, unit), bf16),
+            pltpu.VMEM((1, width), f32),
+            pltpu.VMEM((2, rows, unit), bf16),
+            pltpu.VMEM((rows, 2 * unit), bf16),
+            pltpu.VMEM((rows, unit), f32),
+            pltpu.VMEM((rows, unit), f32),
+            pltpu.VMEM((3, rows, unit), bf16),
+            pltpu.VMEM((3, rows, unit), bf16),
+            dma((2,)),
+            dma((4, 4, n)),
+            dma((4, n)),
+            dma((2,)),
+            dma((2,)),
+            dma((4,)),
+            dma((1,)),
+            dma((3,)),
+            dma((3,)),
+        ],
+        compiler_params=pltpu.CompilerParams(
+            collective_id=0, has_side_effects=True, vmem_limit_bytes=48 * 1024 * 1024
+        ),
+    )(*args)
 
 
 def passed_along(value, axis, steps):
@@ -117,8 +485,17 @@
         P("section", "ctx", None),
         P("section", None, "ctx"),
     )
+    def local(*args):
+        rows, width = args[0].shape[1:]
+        unit = args[2].shape[2]
+        n = mesh.shape["ctx"]
+        even = n % 4 == 0 and n <= 16 and mesh.shape["section"] > 1
+        if even and rows == unit == 2 * HEAD and width == n * unit and rows % 32 == 0:
+            return fused(mesh, *args)
+        return per_device(*args)
+
     return jax.shard_map(
-        per_device,
+        local,
         mesh=mesh,
         in_specs=placed,
         out_specs=(

time: 174 us -> 97 us (0.56)
  waiting for transfers between devices: 129 us -> 0 us
  Pallas kernels: 0 us -> 82 us
  between operations: 13.9 us -> 0.67 us
  matrix products: 11.4 us -> 0 us
  local copies, waits for them, and re-layouts: 5.7 us -> 13.9 us
  starting transfers between devices: 7.87 us -> 0 us
  other arithmetic: 6.42 us -> 0 us
    pallas_call x0 -> x1, Pallas kernels: none -> 82 us  [fused(): pl.pallas_call(functools.partial(kernel, sections, n), out_shape=(jax.Sha...]
    all_gather x3 -> x0, waiting for transfers between devices: 78 us -> none  [the longest x1 39 us: per_device(): query_sum = add_one(lax.all_gather(w_query[0], 'ctx', axis=0, tiled=True))]
    ppermute x3 -> x0, waiting for transfers between devices: 48.5 us -> none  [passed_along(): return lax.ppermute(value, axis, pairs)]
    dot_general x9 -> x0, matrix products: 11.4 us -> none  [the longest x2 5.87 us: add_rows(): return jnp.dot(normed, shard_rows, preferred_element_type=jnp.float32)]
    unnamed x14 -> x22, local copies, waits for them, and re-layouts: 2.27 us -> 12.5 us
    ppermute x3 -> x0, starting transfers between devices: 7.75 us -> none  [passed_along(): return lax.ppermute(value, axis, pairs)]
    add x3 -> x0, other arithmetic: 3.91 us -> none  [the longest x2 3.89 us: device_positions(): return span_index * half_rows + offsets % half_rows]
    unnamed x3 -> x0, waiting for transfers between devices: 2.06 us -> none
  transfers between devices with their start and end apart: 6 -> 0, of which waited for: 4 -> 0; matrix products, arithmetic and copies ran while one was open for 10% -> 0% of each run, Pallas kernels for 0% -> 0%
where the time goes in v1:
time: 97 us; the launch traced here: 96.5 us
  Pallas kernels  82 us (85%)
  local copies, waits for them, and re-layouts  13.9 us (14%)
    pallas_call x1, Pallas kernels, fused(): pl.pallas_call(functools.partial(kernel, sections, n), out_shape=(jax.Sha...  82 us
    unnamed x22, local copies, waits for them, and re-layouts  12.5 us

profile of v1, /device:TPU:0, one launch (start us, length us, event | category | flops | bytes accessed | tf_op | source)
XLA Modules:
  0.0 96.5 jit_solution(7796923112718235575)
XLA Ops:
  0.6 0.8 copy.18.span_ref
  1.4 0.8 copy.16.max_ref
  2.2 0.8 copy.17.sum_ref
  3.0 0.0 copy-start
  3.0 1.6 %copy-done = bf16[1,256,4096]{2,1,0:T(8,128)(2,1)S(1)} copy-done((bf16[1,256,4096]{2,1,0:T(8,128)(2,1)S(1)}, bf16[1,256,4096]{2,1,0:T(8,128)(2,1)}, u32[]{:S(2)}) %copy-start) | copy-done | bytes 2097176
  4.6 0.0 copy-start.1
  4.6 1.0 %copy-done.1 = f32[1,256,512]{2,1,0:T(8,128)S(1)} copy-done((f32[1,256,512]{2,1,0:T(8,128)S(1)}, f32[1,256,512]{2,1,0:T(8,128)}, u32[]{:S(2)}) %copy-start.1) | copy-done | bytes 524312
  5.7 0.0 copy-start.2
  5.7 0.9 copy-done.2
  6.6 0.0 copy-start.3
  6.6 0.9 copy-done.3
  7.6 0.0 copy-start.4
  7.6 0.9 copy-done.4
  8.5 0.0 copy-start.5
  8.5 0.9 copy-done.5
  9.4 0.0 copy-start.6
  9.4 0.9 copy-done.6
  10.3 0.0 copy-start.7
  10.3 0.7 copy-done.7
  11.1 82.0 %shard_map.146 = (bf16[1,256,512]{2,1,0:T(8,128)(2,1)S(1)}, bf16[1,256,256]{2,1,0:T(8,128)(2,1)S(1)}, f32[1,256,4]{2,1,0:T(8,128)S(1)}, f32[1,256,4]{2,1,0:T(8,128)S(1)}, f32[1,256,512]{2,1,0:T(8,128)S(1)}) custom-call(bf16[1,256,4096]{2,1,0:T(8,128)(2,1)S(1)} %copy-done, bf16[1,256,512]{2,1,0:T(8,128)(2,1)S(1)} %copy-done.2, ...), custom_call_target="tpu_custom_call" | custom-call | tf_op jit(solution)/shard_map/pallas_call | solution.py:339
  93.0 0.7 copy.19
  93.7 0.7 copy.20
  94.4 0.7 copy.24
  95.1 0.7 copy.25
  95.7 0.8 copy.26
Async XLA Ops:
  3.0 1.6 %copy-start = (bf16[1,256,4096]{2,1,0:T(8,128)(2,1)S(1)}, bf16[1,256,4096]{2,1,0:T(8,128)(2,1)}, u32[]{:S(2)}) copy-start(bf16[1,256,4096]{2,1,0:T(8,128)(2,1)} %resid_hbm.1) | copy-start | bytes 6291460
  4.6 1.0 %copy-start.1 = (f32[1,256,512]{2,1,0:T(8,128)S(1)}, f32[1,256,512]{2,1,0:T(8,128)}, u32[]{:S(2)}) copy-start(f32[1,256,512]{2,1,0:T(8,128)} %run_ref.1) | copy-start | bytes 1572868
  5.7 0.9 copy-start.2
  6.6 0.9 copy-start.3
  7.6 0.9 copy-start.4
  8.5 0.9 copy-start.5
  9.4 0.9 copy-start.6
  10.3 0.7 copy-start.7

commit v2 on v1

--- a/solution.py
+++ b/solution.py
@@ -12,6 +12,59 @@
 MESH = pl.DeviceIdType.MESH
 CORE, ACROSS, UP, DOWN = range(4)
 OUT, KV, QA, QB = range(4)
+ACROSS_FIRST = QB
+ATTEND, PROJECT, NORMALISE, FINISH = range(10, 14)
+
+ORDER = [(OUT,0,0),(QB,0,0),(KV,0,0),(QA,0,0),(ATTEND,),(OUT,1,0),(OUT,0,1),(QB,0,1),(OUT,2,0),(OUT,1,1),(KV,1,0),(KV,0,1),(QB,1,0),(QA,1,0),(QA,0,1),(OUT,3,0),(OUT,2,1),(KV,2,0),(KV,1,1),(QB,1,1),
+(QA,2,0),(OUT,3,1),(PROJECT,),(KV,3,0),(QB,2,0),(QA,1,1),(QA,3,0),(NORMALISE,),(KV,2,1),(KV,3,1),(FINISH,KV),(QB,2,1),(QA,2,1),(QA,3,1),(FINISH,QA),(QB,3,0),(QB,3,1),(FINISH,QB),]
+
+
+def places(span_ref, rows):
+    half = rows // 2
+    row = lax.broadcasted_iota(jnp.int32, (rows, 1), 0)
+    col = lax.broadcasted_iota(jnp.int32, (1, rows), 1)
+
+    def position(device, offsets):
+        first, second = span_ref[0, device], span_ref[1, device]
+        return jnp.where(offsets < half, first * half + offsets, second * half + offsets - half)
+
+    return row, col, position
+
+
+def column(ref, h):
+    return jnp.transpose(ref[0, h:h + 1, :])
+
+
+def update(query, key, value, keep, m, l, acc):
+    scores = lax.dot_general(
+        query, key, (((1,), (1,)), ((), ())), preferred_element_type=jnp.float32
+    ) * HEAD ** (-0.5)
+    masked = jnp.where(keep, scores, -1e30)
+    top = jnp.max(masked, axis=1, keepdims=True)
+    m_new = top if m is None else jnp.maximum(m, top)
+    p = jnp.where(keep, jnp.exp(scores - m_new), 0.0)
+    l_new = jnp.sum(p, axis=1, keepdims=True)
+    out = jnp.dot(p.astype(jnp.bfloat16), value, preferred_element_type=jnp.float32)
+    if m is not None:
+        decay = jnp.exp(m - m_new)
+        l_new = l * decay + l_new
+        out = acc * decay + out
+    return m_new, l_new, out
+
+
+def own_kernel(span_ref, in_buf, q_out, kv_out, max_out, sum_out, out_out):
+    me = lax.axis_index("ctx")
+    rows, unit = in_buf.shape[1:]
+    row, col, position = places(span_ref, rows)
+    keep = position(me, col) <= position(me, row)
+    kv_out[0] = in_buf[0]
+    for h in range(QHEADS):
+        query = in_buf[1 + h // 2, :, (h % 2) * HEAD:(h % 2 + 1) * HEAD]
+        m, l, acc = update(query, in_buf[0, :, :HEAD], in_buf[0, :, HEAD:], keep, None, None, None)
+        q_out[0, :, h * HEAD:(h + 1) * HEAD] = query
+        max_out[0, h:h + 1, :] = jnp.transpose(m)
+        sum_out[0, h:h + 1, :] = jnp.transpose(l)
+        out_out[0, :, h * HEAD:(h + 1) * HEAD] = acc
 
 
 def kernel(
@@ -28,11 +81,7 @@
     wq_hbm,
     wkv_hbm,
     wo_hbm,
-    q_out,
-    kv_out,
-    max_out,
-    sum_out,
-    out_out,
+    in_buf,
     wo_buf,
     w_buf,
     resid_buf,
@@ -43,7 +92,6 @@
     acc_buf,
     sq_buf,
     ship_buf,
-    in_buf,
     local_sem,
     send_sem,
     recv_sem,
@@ -61,7 +109,6 @@
     ahead = lax.rem(sec + 1, sections)
     behind = lax.rem(sec + sections - 1, sections)
     rows = resid_buf.shape[0]
-    half = rows // 2
     unit = w_buf.shape[-1]
 
     load_resid = pltpu.make_async_copy(resid_hbm.at[0], resid_buf, local_sem.at[0])
@@ -118,8 +165,10 @@
                    (QB, wq_hbm.at[0, :, unit:2 * unit])):
         swaps.append(remote(ref, slot(u, me), xsend_sem.at[u], recv_sem.at[u, me], (behind, me)))
     gain_copy = remote(gain_hbm, gain_buf, xsend_sem.at[0], gain_sem.at[0], (behind, me))
+    swaps[2].start()
     swaps[0].start()
     gain_copy.start()
+    swaps[1].start()
 
     def hop(u, src, way):
         target = {
@@ -149,8 +198,8 @@
                 else:
                     act(hop(u, src, way))
 
-        onward = u == KV or not other
-        across = [ACROSS] if (not other and (u != KV or d == 0)) else []
+        onward = u == ACROSS_FIRST or not other
+        across = [ACROSS] if (not other and (u != ACROSS_FIRST or d == 0)) else []
         if d == 0:
             go(index(z, yy, c), ([UP, DOWN] if onward else []) + across + [CORE])
         else:
@@ -168,66 +217,19 @@
                  None if own else lambda src: arrive(u, src))
 
     load_out.wait()
-    event(OUT, 0, False)
-    swaps[1].start()
-    swaps[2].start()
-
-    row = lax.broadcasted_iota(jnp.int32, (rows, 1), 0)
-    col = lax.broadcasted_iota(jnp.int32, (1, rows), 1)
-
-    def position(device, offsets):
-        first, second = span_ref[device, 0], span_ref[device, 1]
-        return jnp.where(offsets < half, first * half + offsets, second * half + offsets - half)
-
+
+    row, col, position = places(span_ref, rows)
     pos_mine = position(me, row)
-
-    def update(query, key, value, keep, m, l, acc):
-        scores = lax.dot_general(
-            query, key, (((1,), (1,)), ((), ())), preferred_element_type=jnp.float32
-        ) * HEAD ** (-0.5)
-        masked = jnp.where(keep, scores, -1e30)
-        top = jnp.max(masked, axis=1, keepdims=True)
-        m_new = top if m is None else jnp.maximum(m, top)
-        p = jnp.where(keep, jnp.exp(scores - m_new), 0.0)
-        l_new = jnp.sum(p, axis=1, keepdims=True)
-        out = jnp.dot(p.astype(jnp.bfloat16), value, preferred_element_type=jnp.float32)
-        if m is not None:
-            decay = jnp.exp(m - m_new)
-            l_new = l * decay + l_new
-            out = acc * decay + out
-        return m_new, l_new, out
-
-    far_copy.wait_recv()
-    near_copy.wait_recv()
     keep_far = position(lax.rem(me + 2, n), col) <= pos_mine
     keep_near = position(lax.rem(me + 1, n), col) <= pos_mine
 
     def attend(h):
         cols = slice(h * HEAD, (h + 1) * HEAD)
         query = queries_ref[0, :, cols]
-        m, l, acc = max_ref[0, :, h:h + 1], sum_ref[0, :, h:h + 1], run_ref[0, :, cols]
+        m, l, acc = column(max_ref, h), column(sum_ref, h), run_ref[0, :, cols]
         m, l, acc = update(query, near_buf[1, :, :HEAD], near_buf[1, :, HEAD:], keep_far, m, l, acc)
         m, l, acc = update(query, near_buf[0, :, :HEAD], near_buf[0, :, HEAD:], keep_near, m, l, acc)
         att_buf[:, cols] = (acc / l).astype(jnp.bfloat16)
-
-    for h in range(QHEADS):
-        attend(h)
-
-    event(KV, 0, False)
-    event(OUT, 1, False)
-    event(OUT, 0, True)
-    event(KV, 0, True)
-    load_resid.wait()
-    event(OUT, 2, False)
-    event(OUT, 1, True)
-    event(OUT, 3, False)
-    event(QA, 0, False)
-    event(KV, 1, False)
-    event(OUT, 2, True)
-    event(KV, 1, True)
-    event(OUT, 3, True)
-
-    sq_buf[...] = jnp.zeros_like(sq_buf)
 
     def project(step, carry):
         src = lax.rem(me + step, n)
@@ -244,27 +246,11 @@
         sq_buf[...] += wide * wide
         return carry
 
-    lax.fori_loop(0, n, project, 0)
-    gain_copy.wait_recv()
-    mean_square = jnp.sum(sq_buf[...], axis=1, keepdims=True) * (1.0 / (n * unit))
-    inverse = lax.rsqrt(mean_square + 1e-05)
-
-    def normalise(src, carry):
+    def normalise(inverse, src, carry):
         at = pl.ds(pl.multiple_of(src * unit, unit), unit)
         wide = fin_buf[src].astype(jnp.float32)
         fin_buf[src] = (wide * inverse * gain_buf[:, at]).astype(jnp.bfloat16)
         return carry
-
-    event(KV, 2, False)
-    event(KV, 2, True)
-    event(QA, 1, False)
-    event(QB, 0, False)
-    lax.fori_loop(0, n, normalise, 0)
-    event(KV, 3, False)
-    event(KV, 3, True)
-    event(QA, 0, True)
-    event(QA, 2, False)
-    event(QA, 1, True)
 
     def finish(u):
         acc_buf[...] = jnp.zeros_like(acc_buf)
@@ -284,36 +270,28 @@
         copy.start()
         return copy
 
-    results = [finish(KV)]
-    event(QA, 3, False)
-    event(QB, 1, False)
-    event(QA, 2, True)
-    event(QB, 0, True)
-    event(QB, 2, False)
-    event(QA, 3, True)
-    event(QB, 1, True)
-    event(QB, 3, False)
-    results.append(finish(QA))
-    event(QB, 2, True)
-    event(QB, 3, True)
-    results.append(finish(QB))
-
-    keep_own = position(me, col) <= pos_mine
-
-    def own(h):
-        query = in_buf[1 + h // 2, :, (h % 2) * HEAD:(h % 2 + 1) * HEAD]
-        m, l, acc = update(query, in_buf[0, :, :HEAD], in_buf[0, :, HEAD:], keep_own, None, None, None)
-        max_out[0, :, h:h + 1] = m
-        sum_out[0, :, h:h + 1] = l
-        out_out[0, :, h * HEAD:(h + 1) * HEAD] = acc
-
-    results[0].wait_recv()
-    kv_out[0] = in_buf[0]
-    for pair in range(2):
-        results[1 + pair].wait_recv()
-        q_out[0, :, pair * unit:(pair + 1) * unit] = in_buf[1 + pair]
-        own(2 * pair)
-        own(2 * pair + 1)
+    results = []
+    for step in ORDER:
+        if step[0] < ATTEND:
+            event(step[0], step[1], step[2] == 1)
+        elif step[0] == ATTEND:
+            far_copy.wait_recv()
+            near_copy.wait_recv()
+            for h in range(QHEADS):
+                attend(h)
+        elif step[0] == PROJECT:
+            load_resid.wait()
+            sq_buf[...] = jnp.zeros_like(sq_buf)
+            lax.fori_loop(0, n, project, 0)
+        elif step[0] == NORMALISE:
+            gain_copy.wait_recv()
+            mean_square = jnp.sum(sq_buf[...], axis=1, keepdims=True) * (1.0 / (n * unit))
+            inverse = lax.rsqrt(mean_square + 1e-05)
+            lax.fori_loop(0, n, functools.partial(normalise, inverse), 0)
+        else:
+            results.append(finish(step[1]))
+    for copy in results:
+        copy.wait_recv()
 
     near_copy.wait_send()
     far_copy.wait_send()
@@ -334,19 +312,15 @@
     bf16, f32 = jnp.bfloat16, jnp.float32
     vmem = pl.BlockSpec(memory_space=pltpu.VMEM)
     smem = pl.BlockSpec(memory_space=pltpu.SMEM)
-    hbm = pl.BlockSpec(memory_space=pl.ANY)
+    hbm = pl.BlockSpec(memory_space=pltpu.HBM)
     dma = pltpu.SemaphoreType.DMA
-    return pl.pallas_call(
+    turned_max, turned_sum = jnp.swapaxes(run_max, 1, 2), jnp.swapaxes(run_sum, 1, 2)
+    turned_span = jnp.swapaxes(args[6], 0, 1)
+    arrived = pl.pallas_call(
         functools.partial(kernel, sections, n),
-        out_shape=(
-            jax.ShapeDtypeStruct(queries.shape, bf16),
-            jax.ShapeDtypeStruct(keyvals.shape, bf16),
-            jax.ShapeDtypeStruct(run_max.shape, f32),
-            jax.ShapeDtypeStruct(run_sum.shape, f32),
-            jax.ShapeDtypeStruct(run_out.shape, f32),
-        ),
+        out_shape=jax.ShapeDtypeStruct((3, rows, unit), bf16),
         in_specs=[hbm, vmem, hbm, vmem, vmem, vmem, smem, hbm, hbm, hbm, hbm],
-        out_specs=[vmem] * 5,
+        out_specs=vmem,
         scratch_shapes=[
             pltpu.VMEM((n, 2 * unit, unit), bf16),
             pltpu.VMEM((3, n, unit, unit), bf16),
@@ -357,7 +331,6 @@
             pltpu.VMEM((rows, 2 * unit), bf16),
             pltpu.VMEM((rows, unit), f32),
             pltpu.VMEM((rows, unit), f32),
-            pltpu.VMEM((3, rows, unit), bf16),
             pltpu.VMEM((3, rows, unit), bf16),
             dma((2,)),
             dma((4, 4, n)),
@@ -370,9 +343,22 @@
             dma((3,)),
         ],
         compiler_params=pltpu.CompilerParams(
-            collective_id=0, has_side_effects=True, vmem_limit_bytes=48 * 1024 * 1024
+            collective_id=0, has_side_effects=True, vmem_limit_bytes=62 * 1024 * 1024
         ),
-    )(*args)
+    )(resid, queries, keyvals, turned_max, turned_sum, run_out, turned_span, *args[7:])
+    q_new, kv_new, max_new, sum_new, out_new = pl.pallas_call(
+        own_kernel,
+        out_shape=(
+            jax.ShapeDtypeStruct(queries.shape, bf16),
+            jax.ShapeDtypeStruct(keyvals.shape, bf16),
+            jax.ShapeDtypeStruct(turned_max.shape, f32),
+            jax.ShapeDtypeStruct(turned_sum.shape, f32),
+            jax.ShapeDtypeStruct(run_out.shape, f32),
+        ),
+        in_specs=[smem, vmem],
+        out_specs=[vmem] * 5,
+    )(turned_span, arrived)
+    return q_new, kv_new, jnp.swapaxes(max_new, 1, 2), jnp.swapaxes(sum_new, 1, 2), out_new
 
 
 def passed_along(value, axis, steps):

time: 97 us -> 82.3 us (0.85)
  local copies, waits for them, and re-layouts: 13.9 us -> 0 us
    unnamed x22 -> x0, local copies, waits for them, and re-layouts: 12.5 us -> none
    pallas_call x2 -> x0, local copies, waits for them, and re-layouts: 1.34 us -> none  [fused(): pl.pallas_call(functools.partial(kernel, sections, n), out_shape=(jax.Sha...]
    pallas_call x1 -> x2, Pallas kernels: 82 us -> 81.5 us  [the longest x1 78.4 us: fused(): pl.pallas_call(functools.partial(kernel, sections, n), out_shape=jax.Shap...]
where the time goes in v2:
time: 82.3 us; the launch traced here: 82.1 us
  Pallas kernels  81.5 us (99%)
    pallas_call x1, Pallas kernels, fused(): pl.pallas_call(functools.partial(kernel, sections, n), out_shape=jax.Shap...  78.4 us
    pallas_call x1, Pallas kernels, fused(): pl.pallas_call(own_kernel, out_shape=(jax.ShapeDtypeStruct(queries.shape,...  3.1 us

profile of v2, /device:TPU:0, one launch (start us, length us, event | category | flops | bytes accessed | tf_op | source)
XLA Modules:
  0.0 82.1 jit_solution(34666017464529235)
XLA Ops:
  0.6 78.4 %shard_map.146.in_buf = bf16[3,256,256]{2,1,0:T(8,128)(2,1)} custom-call(bf16[1,256,4096]{2,1,0:T(8,128)(2,1)} %resid_hbm.1, bf16[1,256,512]{2,1,0:T(8,128)(2,1)} %queries_ref.1, bf16[1,256,256]{2,1,0:T(8,128)(2,1)} %keyvals_hbm.1, f32[1,4,256]{2,1,0:T(4,128)} %bitcast.5, f32[1,4,256]{2,1,0:T(4,128)} %bitcast.6, f32[1,256,512]{2,1,0:T(8,128)} %run_ref.1, ...), custom_call_target="tpu_custom_call" | custom-call | tf_op jit(solution)/shard_map/pallas_call | solution.py:319
  79.0 3.1 %shard_map.147 = (bf16[1,256,512]{2,1,0:T(8,128)(2,1)}, bf16[1,256,256]{2,1,0:T(8,128)(2,1)}, f32[1,4,256]{2,1,0:T(4,128)}, f32[1,4,256]{2,1,0:T(4,128)}, f32[1,256,512]{2,1,0:T(8,128)}) custom-call(s32[2,16]{1,0:T(2,128)} %bitcast.8, bf16[3,256,256]{2,1,0:T(8,128)(2,1)} %shard_map.146.in_buf), custom_call_target="tpu_custom_call" | custom-call | tf_op jit(solution)/shard_map/pallas_call | solution.py:349
